TPU v7x, 512 devices: a whole 4x4x16 slice. The times are simulated.
512 devices in a mesh: tile: 32 (over y, x, core), aux: 16 (over z).
Axes of the slice: x: 4, y: 4, z: 16, core: 2. Of those that a mesh axis runs over, the one named last changes fastest.
Arguments:
- amplitudes: bfloat16 [128, 128, 128], P('tile'), may hold values from -6 to 6
- df_factors: bfloat16 [1536, 3072], P('aux'), may hold values from -0.15625 to 0.15625
- out_tiles: int32 [1024], P(('tile', 'aux')), may hold values from 0 to 23
- pair_col: int32 [1024, 16], P(('tile', 'aux')), may hold values from 0 to 23
- pair_amp: int32 [1024, 16], replicated, may hold values from 0 to 127, as said below
Outputs:
- residual: bfloat16 [1024, 128, 128], P(('tile', 'aux'))
Inputs may be any that keep to these rules, and one draw needn't show every extreme that they name: `pair_amp`: among the 32 entries of the output tiles of one device, no owner occurs more than 2 times, and in every device's entries at least one owner occurs exactly 2 times (several may).
All inputs are finite; a program needn't handle non-finite values.
Results may differ from a plain program's by a relative error of at most 0.0049.
Values may be sent and summed in bfloat16 or wider, within the bound.
A program may use at most 128 MiB of HBM per device.

v0:
```python
import jax
import jax.numpy as jnp
from jax import lax
from jax.sharding import PartitionSpec as P


def body(amplitudes, df_factors, out_tiles, pair_col, pair_amp):
    n_tile = lax.axis_size("tile")
    n_aux = lax.axis_size("aux")
    me_tile = lax.axis_index("tile")
    me_aux = lax.axis_index("aux")
    out_count = out_tiles.shape[0]
    pair_count = pair_col.shape[1]
    tile_size = amplitudes.shape[1]
    pair_width = df_factors.shape[1]
    ptiles = pair_width // tile_size
    per_device = out_count * pair_count
    shard_rows = lax.all_gather(df_factors, "aux", axis=0, tiled=True)
    columns = shard_rows.reshape(shard_rows.shape[0], ptiles, tile_size)
    right_side = jnp.take(columns, out_tiles, axis=1)
    assembled = jnp.einsum(
        "qv,qob->ovb", shard_rows, right_side, preferred_element_type=jnp.float32
    )
    gram_rows = assembled.reshape(out_count, ptiles, tile_size, tile_size)
    panels = jnp.take_along_axis(gram_rows, pair_col[:, :, None, None], axis=1).astype(jnp.bfloat16)
    everyone = pair_amp.reshape(n_tile, n_aux, per_device)
    my_lists = lax.dynamic_index_in_dim(everyone, me_aux, 1, keepdims=False)
    own_list = lax.dynamic_index_in_dim(my_lists, me_tile, 0, keepdims=False)
    all_tiles = lax.all_gather(amplitudes, "tile", axis=0, tiled=True)
    picked = jnp.take(all_tiles, own_list, axis=0)
    stacked = picked.reshape(out_count, pair_count, tile_size, tile_size)
    result = jnp.einsum("okac,okcb->oab", stacked, panels, preferred_element_type=jnp.float32)
    return result.astype(jnp.bfloat16)


def solution(mesh):
    in_specs = (
        P("tile", None, None),
        P("aux", None),
        P(("tile", "aux")),
        P(("tile", "aux"), None),
        P(),
    )
    out_specs = P(("tile", "aux"), None, None)
    return jax.shard_map(body, mesh=mesh, in_specs=in_specs, out_specs=out_specs, check_vma=False)
```

profile of v0, /device:TPU:1, one launch (start us, length us, event | category | flops | bytes accessed | tf_op | source)
XLA Modules:
  0.0 227.0 jit_solution(2826224950712772218)
XLA Ops:
  6.5 0.0 all-gather.3.cloned.1.call-start
  6.5 0.7 all-gather.3.cloned.1.call-update
  7.3 0.0 all-gather.5.cloned.1.call-start
  7.3 0.7 all-gather.5.cloned.1.call-update
  8.0 0.7 bitcast_or_fusion
  8.7 0.1 reshape.94
  8.8 1.0 copy.11
  9.8 0.1 reshape.74
  10.0 0.1 squeeze.8
  10.1 0.7 compare_select_fusion.2
  10.8 0.7 compare_and_fusion
  11.4 0.7 compare_and_fusion.1
  12.1 65.5 %all-gather.3.cloned.1.call-done = bf16[128,128,128]{2,1,0:T(8,128)(2,1)} async-done(((bf16[4,128,128]{2,1,0:T(8,128)(2,1)}), bf16[128,128,128]{2,1,0:T(8,128)(2,1)}) %all-gather.3.cloned.1.call-update) | async-done | bytes 4194320 | tf_op jit(solution)/shard_map/all_gather | solution.py:29
  77.6 3.9 %gather_fusion = bf16[32,128,128]{2,1,0:T(8,128)(2,1)} fusion(bf16[128,128,128]{2,1,0:T(8,128)(2,1)} %all-gather.3.cloned.1.call-done, s32[1024]{0:T(1024)S(1)} %pad_clamp_fusion.1), kind=kCustom, calls=%fused_computation | custom fusion | bytes 2097280 | tf_op jit(solution)/shard_map/jit(_take)/gather | solution.py:30
  81.5 113.8 %all-gather.5.cloned.1.call-done = bf16[1536,3072]{1,0:T(8,128)(2,1)} async-done(((bf16[96,3072]{1,0:T(8,128)(2,1)}), bf16[1536,3072]{1,0:T(8,128)(2,1)}) %all-gather.5.cloned.1.call-update) | async-done | bytes 9437200 | tf_op jit(solution)/shard_map/all_gather | solution.py:18
  195.3 9.9 %copy_bitcast_fusion = bf16[1536,24,128]{2,0,1:T(8,128)(2,1)} fusion(bf16[1536,3072]{1,0:T(8,128)(2,1)} %all-gather.5.cloned.1.call-done), kind=kLoop, calls=%fused_computation.3 | loop fusion | bytes 18874368 | tf_op jit(solution)/shard_map/reshape | solution.py:19
  205.2 4.4 %gather_fusion.1 = bf16[2,1536,128]{2,1,0:T(8,128)(2,1)S(1)} fusion(bf16[1536,24,128]{2,0,1:T(8,128)(2,1)} %copy_bitcast_fusion, s32[1024]{0:T(1024)S(1)} %pad_clamp_fusion), kind=kCustom, calls=%fused_computation.1 | custom fusion | bytes 1572872 | tf_op jit(solution)/shard_map/jit(_take)/gather | solution.py:20
  209.6 6.5 %fusion.2 = bf16[2,3072,128]{1,2,0:T(8,128)(2,1)S(1)} fusion(bf16[1536,3072]{1,0:T(8,128)(2,1)} %all-gather.5.cloned.1.call-done, bf16[2,1536,128]{2,1,0:T(8,128)(2,1)S(1)} %gather_fusion.1, pred[2]{0:T(512)(128)(4,1)S(1)} %compare_and_fusion), kind=kOutput, calls=%fused_computation.6 | convolution fusion | flops 2416312320 | bytes 11796482 | tf_op jit(solution)/shard_map/qv,qob->ovb/dot_general | solution.py:21
  216.1 0.9 copy.17
  217.0 0.8 gather_fusion.2
  217.8 2.4 %fusion.5 = bf16[2,128,128]{2,1,0:T(8,128)(2,1)} fusion(bf16[2,16,128,128]{3,2,1,0:T(8,128)(2,1)S(1)} %bitcast.33, bf16[2,16,128,128]{3,2,1,0:T(8,128)(2,1)} %bitcast.32, pred[2,16]{1,0:T(4,128)(4,1)S(1)} %get-tuple-element.5, pred[2,16]{1,0:T(4,128)(4,1)S(1)} %get-tuple-element.6), kind=kOutput, calls=%fused_computation.9 | convolution fusion | flops 135299072 | bytes 2162752 | tf_op jit(solution)/shard_map/okac,okcb->oab/dot_general | solution.py:32
  (4 shorter events, 0.0 us)
Async XLA Ops:
  6.5 71.1 %all-gather.3.cloned.1.call-start = ((), (), s32[]{:S(2)}) async-start(), calls=%async_computation | async-start | bytes 4325376 | tf_op jit(solution)/shard_map/all_gather | solution.py:29
  7.3 188.0 %all-gather.5.cloned.1.call-start = ((), (), s32[]{:S(2)}) async-start(), calls=%async_computation.1 | async-start | bytes 10027008 | tf_op jit(solution)/shard_map/all_gather | solution.py:18
Sparse Core Ops, SparseCore 0:
  10.5 67.0 all-gather.2
  79.7 115.5 all-gather.4
where the time goes:
time: 227 us
  waiting for transfers between devices  181 us (80%)
  local copies, waits for them, and re-layouts  21.2 us (9%)
  between operations  13.5 us (6%)
  matrix products  8.9 us (4%)
  other arithmetic  2.72 us (1%)
    all_gather x1, waiting for transfers between devices, body(): shard_rows = lax.all_gather(df_factors, 'aux', axis=0, tiled=True)  114 us
    all_gather x1, waiting for transfers between devices, body(): all_tiles = lax.all_gather(amplitudes, 'tile', axis=0, tiled=True)  65.5 us
    reshape x1, local copies, waits for them, and re-layouts, body(): columns = shard_rows.reshape(shard_rows.shape[0], ptiles, tile_size)  9.91 us
    dot_general x1, matrix products, body(): jnp.einsum('qv,qob->ovb', shard_rows, right_side, preferred_element_type=...  6.51 us
  transfers between devices with their start and end apart: 2, of which 2 were waited for; matrix products, arithmetic and copies ran while one was open for 3% of the time, Pallas kernels for 0%

commit v1 on v0

--- a/solution.py
+++ b/solution.py
@@ -2,6 +2,17 @@
 import jax.numpy as jnp
 from jax import lax
 from jax.sharding import PartitionSpec as P
+
+
+def ring_gather(value, axis, dim):
+    ways = lax.axis_size(axis)
+    pieces = [value]
+    for far in range(1, ways):
+        pieces.append(
+            lax.ppermute(pieces[far - 1], axis, [(d, (d - 1) % ways) for d in range(ways)])
+        )
+    line = jnp.concatenate(pieces, axis=dim)
+    return jnp.roll(line, lax.axis_index(axis) * value.shape[dim], axis=dim)
 
 
 def body(amplitudes, df_factors, out_tiles, pair_col, pair_amp):
@@ -15,7 +26,7 @@
     pair_width = df_factors.shape[1]
     ptiles = pair_width // tile_size
     per_device = out_count * pair_count
-    shard_rows = lax.all_gather(df_factors, "aux", axis=0, tiled=True)
+    shard_rows = ring_gather(df_factors, "aux", 0)
     columns = shard_rows.reshape(shard_rows.shape[0], ptiles, tile_size)
     right_side = jnp.take(columns, out_tiles, axis=1)
     assembled = jnp.einsum(

time: 227 us -> 343 us (1.51)
  the two profiles are of different devices: /device:TPU:1 before, /device:TPU:4 now
where the time goes in v1:
time: 343 us; the launch traced here: 341 us
  waiting for transfers between devices  127 us (37%)
  local copies, waits for them, and re-layouts  97.2 us (28%)
  starting transfers between devices  89.8 us (26%)
  between operations  13.6 us (4%)
  matrix products  8.95 us (3%)
  other arithmetic  4.55 us (1%)
    ppermute x15, waiting for transfers between devices, ring_gather(): lax.ppermute(pieces[far - 1], axis, [(d, (d - 1) % ways) for d in range(w...  127 us
    ppermute x15, starting transfers between devices, ring_gather(): lax.ppermute(pieces[far - 1], axis, [(d, (d - 1) % ways) for d in range(w...  89.8 us
    unnamed x48, local copies, waits for them, and re-layouts  44.9 us
    dynamic_slice x2, local copies, waits for them, and re-layouts, ring_gather(): return jnp.roll(line, lax.axis_index(axis) * value.shape[dim], axis=dim)  22.7 us
    reshape x1, local copies, waits for them, and re-layouts, body(): columns = shard_rows.reshape(shard_rows.shape[0], ptiles, tile_size)  12.6 us
  transfers between devices with their start and end apart: 16, of which 15 were waited for; matrix products, arithmetic and copies ran while one was open for 10% of the time, Pallas kernels for 0%

profile of v1, /device:TPU:4, one launch (start us, length us, event | category | flops | bytes accessed | tf_op | source)
XLA Modules:
  0.0 341.1 jit_solution(15573371963661524567)
XLA Ops:
  6.5 11.5 %collective-permute-start = (bf16[96,3072]{1,0:T(8,128)(2,1)}, bf16[96,3072]{1,0:T(8,128)(2,1)S(1)}, u32[]{:S(2)}, u32[]{:S(2)}) collective-permute-start(bf16[96,3072]{1,0:T(8,128)(2,1)} %param.6), channel_id=1, source_target_pairs={{0,15},{1,0},{2,1},{3,2},{4,3},{5,4},{6,5},{7,6},{8,7},{9,8},{10,9... | collective-permute-start | bytes 1769480 | tf_op jit(solution)/shard_map/ppermute | solution.py:12
  18.1 12.9 %collective-permute-done = bf16[96,3072]{1,0:T(8,128)(2,1)S(1)} collective-permute-done((bf16[96,3072]{1,0:T(8,128)(2,1)}, bf16[96,3072]{1,0:T(8,128)(2,1)S(1)}, u32[]{:S(2)}, u32[]{:S(2)}) %collective-permute-start) | collective-permute-done | bytes 589856 | tf_op jit(solution)/shard_map/ppermute | solution.py:12
  31.0 5.5 %collective-permute-start.1 = (bf16[96,3072]{1,0:T(8,128)(2,1)S(1)}, bf16[96,3072]{1,0:T(8,128)(2,1)S(1)}, u32[]{:S(2)}, u32[]{:S(2)}) collective-permute-start(bf16[96,3072]{1,0:T(8,128)(2,1)S(1)} %collective-permute-done), channel_id=1, source_target_pairs={{0,15},{1,0},{2,1},{3,2},{4,3},{5,4},{6,5},{7,6},{8,7},{9,8},{10,9... | collective-permute-start | bytes 1769480 | tf_op jit(solution)/shard_map/ppermute | solution.py:12
  36.4 11.7 %collective-permute-done.1 = bf16[96,3072]{1,0:T(8,128)(2,1)S(1)} collective-permute-done((bf16[96,3072]{1,0:T(8,128)(2,1)S(1)}, bf16[96,3072]{1,0:T(8,128)(2,1)S(1)}, u32[]{:S(2)}, u32[]{:S(2)}) %collective-permute-start.1) | collective-permute-done | bytes 589856 | tf_op jit(solution)/shard_map/ppermute | solution.py:12
  48.1 5.6 %collective-permute-start.2 = (bf16[96,3072]{1,0:T(8,128)(2,1)S(1)}, bf16[96,3072]{1,0:T(8,128)(2,1)S(1)}, u32[]{:S(2)}, u32[]{:S(2)}) collective-permute-start(bf16[96,3072]{1,0:T(8,128)(2,1)S(1)} %collective-permute-done.1), channel_id=1, source_target_pairs={{0,15},{1,0},{2,1},{3,2},{4,3},{5,4},{6,5},{7,6},{8,7},{9,8},{10,9... | collective-permute-start | bytes 1769480 | tf_op jit(solution)/shard_map/ppermute | solution.py:12
  53.8 10.7 %collective-permute-done.2 = bf16[96,3072]{1,0:T(8,128)(2,1)S(1)} collective-permute-done((bf16[96,3072]{1,0:T(8,128)(2,1)S(1)}, bf16[96,3072]{1,0:T(8,128)(2,1)S(1)}, u32[]{:S(2)}, u32[]{:S(2)}) %collective-permute-start.2) | collective-permute-done | bytes 589856 | tf_op jit(solution)/shard_map/ppermute | solution.py:12
  64.5 5.6 %collective-permute-start.3 = (bf16[96,3072]{1,0:T(8,128)(2,1)S(1)}, bf16[96,3072]{1,0:T(8,128)(2,1)S(1)}, u32[]{:S(2)}, u32[]{:S(2)}) collective-permute-start(bf16[96,3072]{1,0:T(8,128)(2,1)S(1)} %collective-permute-done.2), channel_id=1, source_target_pairs={{0,15},{1,0},{2,1},{3,2},{4,3},{5,4},{6,5},{7,6},{8,7},{9,8},{10,9... | collective-permute-start | bytes 1769480 | tf_op jit(solution)/shard_map/ppermute | solution.py:12
  70.1 9.8 %collective-permute-done.3 = bf16[96,3072]{1,0:T(8,128)(2,1)S(1)} collective-permute-done((bf16[96,3072]{1,0:T(8,128)(2,1)S(1)}, bf16[96,3072]{1,0:T(8,128)(2,1)S(1)}, u32[]{:S(2)}, u32[]{:S(2)}) %collective-permute-start.3) | collective-permute-done | bytes 589856 | tf_op jit(solution)/shard_map/ppermute | solution.py:12
  80.0 5.6 %collective-permute-start.4 = (bf16[96,3072]{1,0:T(8,128)(2,1)S(1)}, bf16[96,3072]{1,0:T(8,128)(2,1)S(1)}, u32[]{:S(2)}, u32[]{:S(2)}) collective-permute-start(bf16[96,3072]{1,0:T(8,128)(2,1)S(1)} %collective-permute-done.3), channel_id=1, source_target_pairs={{0,15},{1,0},{2,1},{3,2},{4,3},{5,4},{6,5},{7,6},{8,7},{9,8},{10,9... | collective-permute-start | bytes 1769480 | tf_op jit(solution)/shard_map/ppermute | solution.py:12
  85.5 8.9 %collective-permute-done.4 = bf16[96,3072]{1,0:T(8,128)(2,1)S(1)} collective-permute-done((bf16[96,3072]{1,0:T(8,128)(2,1)S(1)}, bf16[96,3072]{1,0:T(8,128)(2,1)S(1)}, u32[]{:S(2)}, u32[]{:S(2)}) %collective-permute-start.4) | collective-permute-done | bytes 589856 | tf_op jit(solution)/shard_map/ppermute | solution.py:12
  94.5 5.6 %collective-permute-start.5 = (bf16[96,3072]{1,0:T(8,128)(2,1)S(1)}, bf16[96,3072]{1,0:T(8,128)(2,1)}, u32[]{:S(2)}, u32[]{:S(2)}) collective-permute-start(bf16[96,3072]{1,0:T(8,128)(2,1)S(1)} %collective-permute-done.4), channel_id=1, source_target_pairs={{0,15},{1,0},{2,1},{3,2},{4,3},{5,4},{6,5},{7,6},{8,7},{9,8},{10,9... | collective-permute-start | bytes 1769480 | tf_op jit(solution)/shard_map/ppermute | solution.py:12
  100.1 1.9 copy.15
  102.0 1.9 reshape.74
  104.5 3.6 %collective-permute-done.5 = bf16[96,3072]{1,0:T(8,128)(2,1)} collective-permute-done((bf16[96,3072]{1,0:T(8,128)(2,1)S(1)}, bf16[96,3072]{1,0:T(8,128)(2,1)}, u32[]{:S(2)}, u32[]{:S(2)}) %collective-permute-start.5) | collective-permute-done | bytes 589856 | tf_op jit(solution)/shard_map/ppermute | solution.py:12
  108.1 5.7 %collective-permute-start.6 = (bf16[96,3072]{1,0:T(8,128)(2,1)}, bf16[96,3072]{1,0:T(8,128)(2,1)}, u32[]{:S(2)}, u32[]{:S(2)}) collective-permute-start(bf16[96,3072]{1,0:T(8,128)(2,1)} %collective-permute-done.5), channel_id=1, source_target_pairs={{0,15},{1,0},{2,1},{3,2},{4,3},{5,4},{6,5},{7,6},{8,7},{9,8},{10,9... | collective-permute-start | bytes 1769480 | tf_op jit(solution)/shard_map/ppermute | solution.py:12
  115.2 1.2 bitcast_or_fusion
  116.4 5.8 %collective-permute-done.6 = bf16[96,3072]{1,0:T(8,128)(2,1)} collective-permute-done((bf16[96,3072]{1,0:T(8,128)(2,1)}, bf16[96,3072]{1,0:T(8,128)(2,1)}, u32[]{:S(2)}, u32[]{:S(2)}) %collective-permute-start.6) | collective-permute-done | bytes 589856 | tf_op jit(solution)/shard_map/ppermute | solution.py:12
  122.2 5.6 %collective-permute-start.7 = (bf16[96,3072]{1,0:T(8,128)(2,1)}, bf16[96,3072]{1,0:T(8,128)(2,1)}, u32[]{:S(2)}, u32[]{:S(2)}) collective-permute-start(bf16[96,3072]{1,0:T(8,128)(2,1)} %collective-permute-done.6), channel_id=1, source_target_pairs={{0,15},{1,0},{2,1},{3,2},{4,3},{5,4},{6,5},{7,6},{8,7},{9,8},{10,9... | collective-permute-start | bytes 1769480 | tf_op jit(solution)/shard_map/ppermute | solution.py:12
  127.8 1.3 fusion.19
  129.9 1.3 squeeze.8
  131.2 1.3 compare_and_fusion.1
  132.4 1.9 constant_dynamic-update-slice_fusion.31
  134.4 2.9 collective-permute-done.7
  137.3 5.6 %collective-permute-start.8 = (bf16[96,3072]{1,0:T(8,128)(2,1)}, bf16[96,3072]{1,0:T(8,128)(2,1)S(1)}, u32[]{:S(2)}, u32[]{:S(2)}) collective-permute-start(bf16[96,3072]{1,0:T(8,128)(2,1)} %collective-permute-done.7), channel_id=1, source_target_pairs={{0,15},{1,0},{2,1},{3,2},{4,3},{5,4},{6,5},{7,6},{8,7},{9,8},{10,9... | collective-permute-start | bytes 1769480 | tf_op jit(solution)/shard_map/ppermute | solution.py:12
  144.6 9.2 %collective-permute-done.8 = bf16[96,3072]{1,0:T(8,128)(2,1)S(1)} collective-permute-done((bf16[96,3072]{1,0:T(8,128)(2,1)}, bf16[96,3072]{1,0:T(8,128)(2,1)S(1)}, u32[]{:S(2)}, u32[]{:S(2)}) %collective-permute-start.8) | collective-permute-done | bytes 589856 | tf_op jit(solution)/shard_map/ppermute | solution.py:12
  153.8 5.5 %collective-permute-start.9 = (bf16[96,3072]{1,0:T(8,128)(2,1)S(1)}, bf16[96,3072]{1,0:T(8,128)(2,1)S(1)}, u32[]{:S(2)}, u32[]{:S(2)}) collective-permute-start(bf16[96,3072]{1,0:T(8,128)(2,1)S(1)} %collective-permute-done.8), channel_id=1, source_target_pairs={{0,15},{1,0},{2,1},{3,2},{4,3},{5,4},{6,5},{7,6},{8,7},{9,8},{10,9... | collective-permute-start | bytes 1769480 | tf_op jit(solution)/shard_map/ppermute | solution.py:12
  161.0 9.9 %collective-permute-done.9 = bf16[96,3072]{1,0:T(8,128)(2,1)S(1)} collective-permute-done((bf16[96,3072]{1,0:T(8,128)(2,1)S(1)}, bf16[96,3072]{1,0:T(8,128)(2,1)S(1)}, u32[]{:S(2)}, u32[]{:S(2)}) %collective-permute-start.9) | collective-permute-done | bytes 589856 | tf_op jit(solution)/shard_map/ppermute | solution.py:12
  170.9 5.6 %collective-permute-start.10 = (bf16[96,3072]{1,0:T(8,128)(2,1)S(1)}, bf16[96,3072]{1,0:T(8,128)(2,1)S(1)}, u32[]{:S(2)}, u32[]{:S(2)}) collective-permute-start(bf16[96,3072]{1,0:T(8,128)(2,1)S(1)} %collective-permute-done.9), channel_id=1, source_target_pairs={{0,15},{1,0},{2,1},{3,2},{4,3},{5,4},{6,5},{7,6},{8,7},{9,8},{10,9... | collective-permute-start | bytes 1769480 | tf_op jit(solution)/shard_map/ppermute | solution.py:12
  177.4 1.9 constant_dynamic-update-slice_fusion.25
  179.3 10.0 %collective-permute-done.10 = bf16[96,3072]{1,0:T(8,128)(2,1)S(1)} collective-permute-done((bf16[96,3072]{1,0:T(8,128)(2,1)S(1)}, bf16[96,3072]{1,0:T(8,128)(2,1)S(1)}, u32[]{:S(2)}, u32[]{:S(2)}) %collective-permute-start.10) | collective-permute-done | bytes 589856 | tf_op jit(solution)/shard_map/ppermute | solution.py:12
  189.4 5.6 %collective-permute-start.11 = (bf16[96,3072]{1,0:T(8,128)(2,1)S(1)}, bf16[96,3072]{1,0:T(8,128)(2,1)S(1)}, u32[]{:S(2)}, u32[]{:S(2)}) collective-permute-start(bf16[96,3072]{1,0:T(8,128)(2,1)S(1)} %collective-permute-done.10), channel_id=1, source_target_pairs={{0,15},{1,0},{2,1},{3,2},{4,3},{5,4},{6,5},{7,6},{8,7},{9,8},{10,9... | collective-permute-start | bytes 1769480 | tf_op jit(solution)/shard_map/ppermute | solution.py:12
  195.0 1.9 constant_dynamic-update-slice_fusion.24
  196.9 1.9 constant_dynamic-update-slice_fusion.23
  198.8 9.6 %collective-permute-done.11 = bf16[96,3072]{1,0:T(8,128)(2,1)S(1)} collective-permute-done((bf16[96,3072]{1,0:T(8,128)(2,1)S(1)}, bf16[96,3072]{1,0:T(8,128)(2,1)S(1)}, u32[]{:S(2)}, u32[]{:S(2)}) %collective-permute-start.11) | collective-permute-done | bytes 589856 | tf_op jit(solution)/shard_map/ppermute | solution.py:12
  208.4 5.6 %collective-permute-start.12 = (bf16[96,3072]{1,0:T(8,128)(2,1)S(1)}, bf16[96,3072]{1,0:T(8,128)(2,1)S(1)}, u32[]{:S(2)}, u32[]{:S(2)}) collective-permute-start(bf16[96,3072]{1,0:T(8,128)(2,1)S(1)} %collective-permute-done.11), channel_id=1, source_target_pairs={{0,15},{1,0},{2,1},{3,2},{4,3},{5,4},{6,5},{7,6},{8,7},{9,8},{10,9... | collective-permute-start | bytes 1769480 | tf_op jit(solution)/shard_map/ppermute | solution.py:12
  214.0 0.9 constant_dynamic-update-slice_fusion.22
  215.8 10.8 %collective-permute-done.12 = bf16[96,3072]{1,0:T(8,128)(2,1)S(1)} collective-permute-done((bf16[96,3072]{1,0:T(8,128)(2,1)S(1)}, bf16[96,3072]{1,0:T(8,128)(2,1)S(1)}, u32[]{:S(2)}, u32[]{:S(2)}) %collective-permute-start.12) | collective-permute-done | bytes 589856 | tf_op jit(solution)/shard_map/ppermute | solution.py:12
  226.6 5.6 %collective-permute-start.13 = (bf16[96,3072]{1,0:T(8,128)(2,1)S(1)}, bf16[96,3072]{1,0:T(8,128)(2,1)}, u32[]{:S(2)}, u32[]{:S(2)}) collective-permute-start(bf16[96,3072]{1,0:T(8,128)(2,1)S(1)} %collective-permute-done.12), channel_id=1, source_target_pairs={{0,15},{1,0},{2,1},{3,2},{4,3},{5,4},{6,5},{7,6},{8,7},{9,8},{10,9... | collective-permute-start | bytes 1769480 | tf_op jit(solution)/shard_map/ppermute | solution.py:12
  233.9 10.2 %collective-permute-done.13 = bf16[96,3072]{1,0:T(8,128)(2,1)} collective-permute-done((bf16[96,3072]{1,0:T(8,128)(2,1)S(1)}, bf16[96,3072]{1,0:T(8,128)(2,1)}, u32[]{:S(2)}, u32[]{:S(2)}) %collective-permute-start.13) | collective-permute-done | bytes 589856 | tf_op jit(solution)/shard_map/ppermute | solution.py:12
  244.1 5.7 %collective-permute-start.14 = (bf16[96,3072]{1,0:T(8,128)(2,1)}, bf16[96,3072]{1,0:T(8,128)(2,1)}, u32[]{:S(2)}, u32[]{:S(2)}) collective-permute-start(bf16[96,3072]{1,0:T(8,128)(2,1)} %collective-permute-done.13), channel_id=1, source_target_pairs={{0,15},{1,0},{2,1},{3,2},{4,3},{5,4},{6,5},{7,6},{8,7},{9,8},{10,9... | collective-permute-start | bytes 1769480 | tf_op jit(solution)/shard_map/ppermute | solution.py:12
  249.8 0.9 constant_dynamic-update-slice_fusion.18
  250.7 3.9 %gather_fusion = bf16[32,128,128]{2,1,0:T(8,128)(2,1)} fusion(bf16[128,128,128]{2,1,0:T(8,128)(2,1)} %all-gather.2.cloned.1.call-done, s32[1024]{0:T(1024)S(1)} %pad_clamp_fusion.1), kind=kCustom, calls=%fused_computation | custom fusion | bytes 2097280 | tf_op jit(solution)/shard_map/jit(_take)/gather | solution.py:41
  254.6 2.0 constant_dynamic-update-slice_fusion.17
  256.6 0.9 collective-permute-done.14
  257.5 1.9 constant_dynamic-update-slice_fusion.16
  260.3 0.9 constant_dynamic-update-slice_fusion.14
  263.7 0.9 constant_dynamic-update-slice_fusion.10
  264.6 1.9 constant_dynamic-update-slice_fusion.9
  266.6 1.9 constant_dynamic-update-slice_fusion.8
  268.5 1.9 constant_dynamic-update-slice_fusion.7
  270.4 1.9 constant_dynamic-update-slice_fusion.6
  272.4 1.9 constant_dynamic-update-slice_fusion.5
  274.3 1.9 constant_dynamic-update-slice_fusion.4
  276.2 1.9 constant_dynamic-update-slice_fusion.3
  278.2 1.9 constant_dynamic-update-slice_fusion.2
  280.1 1.9 constant_dynamic-update-slice_fusion.1
  282.0 1.9 constant_dynamic-update-slice_fusion
  283.9 10.0 %constant_dynamic-slice_fusion = bf16[1536,3072]{1,0:T(8,128)(2,1)} fusion(bf16[3072,3072]{1,0:T(8,128)(2,1)} %constant_dynamic-update-slice_fusion, s32[]{:T(128)S(6)} %select_n.75), kind=kLoop, calls=%fused_computation.61 | loop fusion | bytes 18874372 | tf_op jit(solution)/shard_map/jit(_roll_dynamic)/dynamic_slice | solution.py:15
  294.0 12.7 %copy.16 = bf16[1536,3072]{0,1:T(8,128)(2,1)} copy(bf16[1536,3072]{1,0:T(8,128)(2,1)} %constant_dynamic-slice_fusion) | data formatting | bytes 18874368 | tf_op jit(solution)/shard_map/jit(_roll_dynamic)/dynamic_slice | solution.py:15
  306.6 12.6 %copy.17 = bf16[1536,24,128]{2,0,1:T(8,128)(2,1)} copy(bf16[1536,24,128]{0,2,1:T(8,128)(2,1)} %bitcast.27) | data formatting | bytes 18874368 | tf_op jit(solution)/shard_map/reshape | solution.py:30
  319.2 4.4 %gather_fusion.1 = bf16[2,1536,128]{2,1,0:T(8,128)(2,1)S(1)} fusion(bf16[1536,24,128]{2,0,1:T(8,128)(2,1)} %copy.17, s32[1024]{0:T(1024)S(1)} %pad_clamp_fusion), kind=kCustom, calls=%fused_computation.1 | custom fusion | bytes 1572872 | tf_op jit(solution)/shard_map/jit(_take)/gather | solution.py:31
  323.6 6.6 %fusion.2 = bf16[2,3072,128]{1,2,0:T(8,128)(2,1)S(1)} fusion(bf16[1536,3072]{1,0:T(8,128)(2,1)} %constant_dynamic-slice_fusion, bf16[2,1536,128]{2,1,0:T(8,128)(2,1)S(1)} %gather_fusion.1, pred[2]{0:T(512)(128)(4,1)S(1)} %compare_and_fusion), kind=kOutput, calls=%fused_computation.5 | convolution fusion | flops 2416312320 | bytes 11796482 | tf_op jit(solution)/shard_map/qv,qob->ovb/dot_general | solution.py:32
  330.2 0.9 copy.22
  331.9 2.4 fusion.5
  (38 shorter events, 14.0 us)
Async XLA Ops:
  6.5 252.9 %copy-start = (bf16[96,3072]{1,0:T(8,128)(2,1)S(1)}, bf16[96,3072]{1,0:T(8,128)(2,1)}, u32[]{:S(2)}) copy-start(bf16[96,3072]{1,0:T(8,128)(2,1)} %param.6) | copy-start | bytes 1769476
  6.5 244.2 %all-gather.2.cloned.1.call-start = ((), (), s32[]{:S(2)}) async-start(), calls=%async_computation | async-start | bytes 4325376 | tf_op jit(solution)/shard_map/all_gather | solution.py:40
  6.5 24.4 %collective-permute-start = (bf16[96,3072]{1,0:T(8,128)(2,1)}, bf16[96,3072]{1,0:T(8,128)(2,1)S(1)}, u32[]{:S(2)}, u32[]{:S(2)}) collective-permute-start(bf16[96,3072]{1,0:T(8,128)(2,1)} %param.6), channel_id=1, source_target_pairs={{0,15},{1,0},{2,1},{3,2},{4,3},{5,4},{6,5},{7,6},{8,7},{9,8},{10,9... | collective-permute-start | bytes 1769480 | tf_op jit(solution)/shard_map/ppermute | solution.py:12
  31.0 17.2 %collective-permute-start.1 = (bf16[96,3072]{1,0:T(8,128)(2,1)S(1)}, bf16[96,3072]{1,0:T(8,128)(2,1)S(1)}, u32[]{:S(2)}, u32[]{:S(2)}) collective-permute-start(bf16[96,3072]{1,0:T(8,128)(2,1)S(1)} %collective-permute-done), channel_id=1, source_target_pairs={{0,15},{1,0},{2,1},{3,2},{4,3},{5,4},{6,5},{7,6},{8,7},{9,8},{10,9... | collective-permute-start | bytes 1769480 | tf_op jit(solution)/shard_map/ppermute | solution.py:12
  48.1 16.4 %collective-permute-start.2 = (bf16[96,3072]{1,0:T(8,128)(2,1)S(1)}, bf16[96,3072]{1,0:T(8,128)(2,1)S(1)}, u32[]{:S(2)}, u32[]{:S(2)}) collective-permute-start(bf16[96,3072]{1,0:T(8,128)(2,1)S(1)} %collective-permute-done.1), channel_id=1, source_target_pairs={{0,15},{1,0},{2,1},{3,2},{4,3},{5,4},{6,5},{7,6},{8,7},{9,8},{10,9... | collective-permute-start | bytes 1769480 | tf_op jit(solution)/shard_map/ppermute | solution.py:12
  64.5 15.4 %collective-permute-start.3 = (bf16[96,3072]{1,0:T(8,128)(2,1)S(1)}, bf16[96,3072]{1,0:T(8,128)(2,1)S(1)}, u32[]{:S(2)}, u32[]{:S(2)}) collective-permute-start(bf16[96,3072]{1,0:T(8,128)(2,1)S(1)} %collective-permute-done.2), channel_id=1, source_target_pairs={{0,15},{1,0},{2,1},{3,2},{4,3},{5,4},{6,5},{7,6},{8,7},{9,8},{10,9... | collective-permute-start | bytes 1769480 | tf_op jit(solution)/shard_map/ppermute | solution.py:12
  80.0 14.5 %collective-permute-start.4 = (bf16[96,3072]{1,0:T(8,128)(2,1)S(1)}, bf16[96,3072]{1,0:T(8,128)(2,1)S(1)}, u32[]{:S(2)}, u32[]{:S(2)}) collective-permute-start(bf16[96,3072]{1,0:T(8,128)(2,1)S(1)} %collective-permute-done.3), channel_id=1, source_target_pairs={{0,15},{1,0},{2,1},{3,2},{4,3},{5,4},{6,5},{7,6},{8,7},{9,8},{10,9... | collective-permute-start | bytes 1769480 | tf_op jit(solution)/shard_map/ppermute | solution.py:12
  94.5 13.6 %collective-permute-start.5 = (bf16[96,3072]{1,0:T(8,128)(2,1)S(1)}, bf16[96,3072]{1,0:T(8,128)(2,1)}, u32[]{:S(2)}, u32[]{:S(2)}) collective-permute-start(bf16[96,3072]{1,0:T(8,128)(2,1)S(1)} %collective-permute-done.4), channel_id=1, source_target_pairs={{0,15},{1,0},{2,1},{3,2},{4,3},{5,4},{6,5},{7,6},{8,7},{9,8},{10,9... | collective-permute-start | bytes 1769480 | tf_op jit(solution)/shard_map/ppermute | solution.py:12
  108.1 14.1 %collective-permute-start.6 = (bf16[96,3072]{1,0:T(8,128)(2,1)}, bf16[96,3072]{1,0:T(8,128)(2,1)}, u32[]{:S(2)}, u32[]{:S(2)}) collective-permute-start(bf16[96,3072]{1,0:T(8,128)(2,1)} %collective-permute-done.5), channel_id=1, source_target_pairs={{0,15},{1,0},{2,1},{3,2},{4,3},{5,4},{6,5},{7,6},{8,7},{9,8},{10,9... | collective-permute-start | bytes 1769480 | tf_op jit(solution)/shard_map/ppermute | solution.py:12
  122.2 15.1 %collective-permute-start.7 = (bf16[96,3072]{1,0:T(8,128)(2,1)}, bf16[96,3072]{1,0:T(8,128)(2,1)}, u32[]{:S(2)}, u32[]{:S(2)}) collective-permute-start(bf16[96,3072]{1,0:T(8,128)(2,1)} %collective-permute-done.6), channel_id=1, source_target_pairs={{0,15},{1,0},{2,1},{3,2},{4,3},{5,4},{6,5},{7,6},{8,7},{9,8},{10,9... | collective-permute-start | bytes 1769480 | tf_op jit(solution)/shard_map/ppermute | solution.py:12
  137.3 16.5 %collective-permute-start.8 = (bf16[96,3072]{1,0:T(8,128)(2,1)}, bf16[96,3072]{1,0:T(8,128)(2,1)S(1)}, u32[]{:S(2)}, u32[]{:S(2)}) collective-permute-start(bf16[96,3072]{1,0:T(8,128)(2,1)} %collective-permute-done.7), channel_id=1, source_target_pairs={{0,15},{1,0},{2,1},{3,2},{4,3},{5,4},{6,5},{7,6},{8,7},{9,8},{10,9... | collective-permute-start | bytes 1769480 | tf_op jit(solution)/shard_map/ppermute | solution.py:12
  153.8 60.2 %copy-start.1 = (bf16[96,3072]{1,0:T(8,128)(2,1)}, bf16[96,3072]{1,0:T(8,128)(2,1)S(1)}, u32[]{:S(2)}) copy-start(bf16[96,3072]{1,0:T(8,128)(2,1)S(1)} %collective-permute-done.8) | copy-start | bytes 1769476
  153.8 17.1 %collective-permute-start.9 = (bf16[96,3072]{1,0:T(8,128)(2,1)S(1)}, bf16[96,3072]{1,0:T(8,128)(2,1)S(1)}, u32[]{:S(2)}, u32[]{:S(2)}) collective-permute-start(bf16[96,3072]{1,0:T(8,128)(2,1)S(1)} %collective-permute-done.8), channel_id=1, source_target_pairs={{0,15},{1,0},{2,1},{3,2},{4,3},{5,4},{6,5},{7,6},{8,7},{9,8},{10,9... | collective-permute-start | bytes 1769480 | tf_op jit(solution)/shard_map/ppermute | solution.py:12
  170.9 43.9 %copy-start.2 = (bf16[96,3072]{1,0:T(8,128)(2,1)}, bf16[96,3072]{1,0:T(8,128)(2,1)S(1)}, u32[]{:S(2)}) copy-start(bf16[96,3072]{1,0:T(8,128)(2,1)S(1)} %collective-permute-done.9) | copy-start | bytes 1769476
  170.9 18.4 %collective-permute-start.10 = (bf16[96,3072]{1,0:T(8,128)(2,1)S(1)}, bf16[96,3072]{1,0:T(8,128)(2,1)S(1)}, u32[]{:S(2)}, u32[]{:S(2)}) collective-permute-start(bf16[96,3072]{1,0:T(8,128)(2,1)S(1)} %collective-permute-done.9), channel_id=1, source_target_pairs={{0,15},{1,0},{2,1},{3,2},{4,3},{5,4},{6,5},{7,6},{8,7},{9,8},{10,9... | collective-permute-start | bytes 1769480 | tf_op jit(solution)/shard_map/ppermute | solution.py:12
  189.4 42.8 %copy-start.3 = (bf16[96,3072]{1,0:T(8,128)(2,1)}, bf16[96,3072]{1,0:T(8,128)(2,1)S(1)}, u32[]{:S(2)}) copy-start(bf16[96,3072]{1,0:T(8,128)(2,1)S(1)} %collective-permute-done.10) | copy-start | bytes 1769476
  189.4 19.0 %collective-permute-start.11 = (bf16[96,3072]{1,0:T(8,128)(2,1)S(1)}, bf16[96,3072]{1,0:T(8,128)(2,1)S(1)}, u32[]{:S(2)}, u32[]{:S(2)}) collective-permute-start(bf16[96,3072]{1,0:T(8,128)(2,1)S(1)} %collective-permute-done.10), channel_id=1, source_target_pairs={{0,15},{1,0},{2,1},{3,2},{4,3},{5,4},{6,5},{7,6},{8,7},{9,8},{10,9... | collective-permute-start | bytes 1769480 | tf_op jit(solution)/shard_map/ppermute | solution.py:12
  208.4 24.6 %copy-start.4 = (bf16[96,3072]{1,0:T(8,128)(2,1)}, bf16[96,3072]{1,0:T(8,128)(2,1)S(1)}, u32[]{:S(2)}) copy-start(bf16[96,3072]{1,0:T(8,128)(2,1)S(1)} %collective-permute-done.11) | copy-start | bytes 1769476
  208.4 18.2 %collective-permute-start.12 = (bf16[96,3072]{1,0:T(8,128)(2,1)S(1)}, bf16[96,3072]{1,0:T(8,128)(2,1)S(1)}, u32[]{:S(2)}, u32[]{:S(2)}) collective-permute-start(bf16[96,3072]{1,0:T(8,128)(2,1)S(1)} %collective-permute-done.11), channel_id=1, source_target_pairs={{0,15},{1,0},{2,1},{3,2},{4,3},{5,4},{6,5},{7,6},{8,7},{9,8},{10,9... | collective-permute-start | bytes 1769480 | tf_op jit(solution)/shard_map/ppermute | solution.py:12
  226.6 23.2 %copy-start.5 = (bf16[96,3072]{1,0:T(8,128)(2,1)}, bf16[96,3072]{1,0:T(8,128)(2,1)S(1)}, u32[]{:S(2)}) copy-start(bf16[96,3072]{1,0:T(8,128)(2,1)S(1)} %collective-permute-done.12) | copy-start | bytes 1769476
  226.6 17.5 %collective-permute-start.13 = (bf16[96,3072]{1,0:T(8,128)(2,1)S(1)}, bf16[96,3072]{1,0:T(8,128)(2,1)}, u32[]{:S(2)}, u32[]{:S(2)}) collective-permute-start(bf16[96,3072]{1,0:T(8,128)(2,1)S(1)} %collective-permute-done.12), channel_id=1, source_target_pairs={{0,15},{1,0},{2,1},{3,2},{4,3},{5,4},{6,5},{7,6},{8,7},{9,8},{10,9... | collective-permute-start | bytes 1769480 | tf_op jit(solution)/shard_map/ppermute | solution.py:12
  244.1 13.4 %collective-permute-start.14 = (bf16[96,3072]{1,0:T(8,128)(2,1)}, bf16[96,3072]{1,0:T(8,128)(2,1)}, u32[]{:S(2)}, u32[]{:S(2)}) collective-permute-start(bf16[96,3072]{1,0:T(8,128)(2,1)} %collective-permute-done.13), channel_id=1, source_target_pairs={{0,15},{1,0},{2,1},{3,2},{4,3},{5,4},{6,5},{7,6},{8,7},{9,8},{10,9... | collective-permute-start | bytes 1769480 | tf_op jit(solution)/shard_map/ppermute | solution.py:12
  306.6 25.2 %copy-start.6 = (pred[2,16]{1,0:T(4,128)(4,1)S(1)}, pred[2,16]{1,0:T(4,128)(4,1)}, u32[]{:S(2)}) copy-start(pred[2,16]{1,0:T(4,128)(4,1)} %get-tuple-element.5) | copy-start | bytes 100
  306.6 25.2 %copy-start.7 = (pred[2,16]{1,0:T(4,128)(4,1)S(1)}, pred[2,16]{1,0:T(4,128)(4,1)}, u32[]{:S(2)}) copy-start(pred[2,16]{1,0:T(4,128)(4,1)} %get-tuple-element.6) | copy-start | bytes 100
Sparse Core Ops, SparseCore 0:
  53.9 55.9 all-gather.1
